TPU v7x, 512 devices: a whole 4x8x8 slice. The times are simulated.
512 devices in a mesh: seq: 64 (over z, y), head: 8 (over x, core).
Axes of the slice: x: 4, y: 8, z: 8, core: 2. Of those that a mesh axis runs over, the one named last changes fastest.
Arguments:
- queries: float32 [16384, 4096], P('seq', 'head'), may hold values from -6 to 6
- keys: float32 [16384, 4096], P('seq', 'head'), may hold values from -6 to 6
- values: float32 [16384, 4096], P('seq', 'head'), may hold values from -6 to 6
- out_grad: float32 [16384, 4096], P('seq', 'head'), may hold values from -0.00390625 to 0.00390625
Outputs:
- grad_queries: float32 [16384, 4096], P('seq', 'head')
- grad_keys: float32 [16384, 4096], P('seq', 'head')
- grad_values: float32 [16384, 4096], P('seq', 'head')
All inputs are finite; a program needn't handle non-finite values.
Results may differ from a plain program's by a relative error of at most 0.00014.
Values sent between devices are 32-bit elements; how exact they have to be, the bound alone decides.
A program may use at most 128 MiB of HBM per device.

v0:
```python
import jax
import jax.numpy as jnp
from jax import lax
from jax.sharding import PartitionSpec as P

DK = 128
GROUP = 256


def carried_in(value, axis, combine, identity, reverse):
    peers, here = (lax.axis_size(axis), lax.axis_index(axis))
    everything = lax.all_gather(value, axis)
    start = jnp.broadcast_to(jnp.asarray(identity, value.dtype), value.shape)

    def step(k, before):
        at = peers - 1 - k if reverse else k
        reached = at > here if reverse else at < here
        new = combine(before, everything[at])
        return jnp.where(reached, new, before)

    return lax.fori_loop(0, peers, step, start)


def add_states(earlier, later):
    return jax.tree.map(lambda left, right: left + right, earlier, later)


def shards(queries, keys, values, out_grad):
    hi = lax.Precision.HIGHEST
    length = queries.shape[0]
    width = queries.shape[1]
    heads = width // DK
    block = min(length, GROUP)
    count = length // block

    def head_major(array):
        return array.reshape(length, heads, DK).transpose(1, 0, 2).reshape(heads, count, block, DK)

    q_blk = head_major(queries)
    k_blk = head_major(keys)
    v_blk = head_major(values)
    g_blk = head_major(out_grad)
    rows = lax.broadcasted_iota(jnp.int32, (block, block), 0)
    cols = lax.broadcasted_iota(jnp.int32, (block, block), 1)
    causal = (rows >= cols).astype(jnp.float32)
    scores = jnp.einsum("hntd,hnsd->hnts", q_blk, k_blk, precision=hi) * causal
    dscores = jnp.einsum("hntd,hnsd->hnts", g_blk, v_blk, precision=hi) * causal
    key_blocks = jnp.einsum("hnsd,hnse->hnde", k_blk, v_blk, precision=hi)
    query_blocks = jnp.einsum("hntd,hnte->hnde", q_blk, g_blk, precision=hi)
    key_local = jnp.sum(key_blocks, axis=1)
    query_local = jnp.sum(query_blocks, axis=1)
    prefix = carried_in(key_local, "seq", add_states, jnp.zeros_like(key_local), False)
    suffix = carried_in(query_local, "seq", add_states, jnp.zeros_like(query_local), True)
    block_rows = lax.broadcasted_iota(jnp.int32, (count, count), 0)
    block_cols = lax.broadcasted_iota(jnp.int32, (count, count), 1)
    earlier_mask = (block_rows > block_cols).astype(jnp.float32)
    later_mask = (block_rows < block_cols).astype(jnp.float32)
    key_running = jnp.einsum("nm,hmde->hnde", earlier_mask, key_blocks, precision=hi)
    query_running = jnp.einsum("nm,hmde->hnde", later_mask, query_blocks, precision=hi)
    forward_state = prefix[:, None] + key_running
    backward_state = suffix[:, None] + query_running
    grad_q = jnp.einsum("hnts,hnsd->hntd", dscores, k_blk, precision=hi)
    grad_q = grad_q + jnp.einsum("hnte,hnde->hntd", g_blk, forward_state, precision=hi)
    grad_k = jnp.einsum("hnts,hntd->hnsd", dscores, q_blk, precision=hi)
    grad_k = grad_k + jnp.einsum("hnse,hnde->hnsd", v_blk, backward_state, precision=hi)
    grad_v = jnp.einsum("hnts,hnte->hnse", scores, g_blk, precision=hi)
    grad_v = grad_v + jnp.einsum("hnsd,hnde->hnse", k_blk, backward_state, precision=hi)

    def token_major(array):
        return array.reshape(heads, length, DK).transpose(1, 0, 2).reshape(length, width)

    return (token_major(grad_q), token_major(grad_k), token_major(grad_v))


def solution(mesh):
    return jax.shard_map(
        shards,
        mesh=mesh,
        in_specs=(P("seq", "head"), P("seq", "head"), P("seq", "head"), P("seq", "head")),
        out_specs=(P("seq", "head"), P("seq", "head"), P("seq", "head")),
        check_vma=False,
    )
```

profile of v0, /device:TPU:6, one launch (start us, length us, event | category | flops | bytes accessed | tf_op | source)
XLA Modules:
  0.0 381.8 jit_solution(189591143816758921)
XLA Ops:
  7.2 1.3 copy.44
  8.5 1.2 copy.39
  9.8 1.3 fusion.18
  11.2 2.8 fusion.3
  14.1 2.1 convolution_multiply_fusion.1
  16.2 2.0 convolution_multiply_fusion
  18.2 138.1 %all-gather.7.cloned.1.call-done = f32[256,128,128]{2,1,0:T(8,128)} async-done(((f32[4,128,128]{2,1,0:T(8,128)}), f32[256,128,128]{2,1,0:T(8,128)}) %all-gather.7.cloned.1.call-update) | async-done | bytes 16777232 | tf_op jit(solution)/shard_map/all_gather | solution.py:12
  156.3 68.5 %while.31 = (s32[]{:T(128)}, f32[4,128,128]{2,1,0:T(8,128)S(1)}, s32[]{:T(128)}, f32[64,4,128,128]{3,2,1,0:T(8,128)}, s32[]{:T(128)}, /*index=5*/s32[]{:T(128)}, s32[]{:T(128)}, s32[]{:T(128)}) while((s32[]{:T(128)}, f32[4,128,128]{2,1,0:T(8,128)S(1)}, s32[]{:T(128)}, f32[64,4,128,128]{3,2,1,0:T(8,128)}, s32[]{:T(128)}, ...), condition=%wide.region_3.4_spmd.clone, body=%wide.region_2.3_spmd.clone.sunk | while | flops 196616 | bytes 786595 | solution.py:21
  157.4 1.0 add_select_fusion.5
  159.5 1.0 add_select_fusion.5
  162.7 1.0 add_select_fusion.5
  165.9 1.0 add_select_fusion.5
  171.2 1.0 add_select_fusion.5
  172.3 1.1 add_select_fusion.5
  173.4 1.0 add_select_fusion.5
  179.8 1.0 add_select_fusion.5
  181.9 1.0 add_select_fusion.5
  185.2 1.0 add_select_fusion.5
  188.4 1.1 add_select_fusion.5
  191.6 1.0 add_select_fusion.5
  192.7 1.0 add_select_fusion.5
  199.1 1.0 add_select_fusion.5
  200.2 1.0 add_select_fusion.5
  214.1 1.1 add_select_fusion.5
  222.7 1.1 add_select_fusion.5
  224.8 2.5 convolution_bitcast_fusion.2
  227.4 2.4 convolution_bitcast_fusion
  229.8 68.3 %all-gather.5.cloned.1.call-done = f32[256,128,128]{2,1,0:T(8,128)} async-done(((f32[4,128,128]{2,1,0:T(8,128)}), f32[256,128,128]{2,1,0:T(8,128)}) %all-gather.5.cloned.1.call-update) | async-done | bytes 16777232 | tf_op jit(solution)/shard_map/all_gather | solution.py:12
  298.1 68.1 %while.30 = (s32[]{:T(128)}, f32[4,128,128]{2,1,0:T(8,128)S(1)}, s32[]{:T(128)}, f32[64,4,128,128]{3,2,1,0:T(8,128)}, s32[]{:T(128)}, /*index=5*/s32[]{:T(128)}) while((s32[]{:T(128)}, f32[4,128,128]{2,1,0:T(8,128)S(1)}, s32[]{:T(128)}, f32[64,4,128,128]{3,2,1,0:T(8,128)}, s32[]{:T(128)}, /*index=5*/s32[]{:T(128)}) %tuple.83), condition=%wide.region_1.0_spmd.clone, body=%wide.region_0.0_spmd.clone.sunk | while | flops 196612 | bytes 786533 | solution.py:21
  366.8 1.8 fusion.1
  368.6 1.3 fusion.2
  371.9 2.1 fusion
  (126 shorter events, 119.2 us)
Async XLA Ops:
  7.2 4.0 %copy-start = (f32[256,512]{1,0:T(8,128)S(1)}, f32[256,512]{1,0:T(8,128)}, u32[]{:S(2)}) copy-start(f32[256,512]{1,0:T(8,128)} %param.9) | copy-start | bytes 1572868
  7.2 149.1 %all-gather.7.cloned.1.call-start = ((), (), s32[]{:S(2)}) async-start(), calls=%async_computation.1 | async-start | bytes 17039360 | tf_op jit(solution)/shard_map/all_gather | solution.py:12
  11.1 286.9 %all-gather.5.cloned.1.call-start = ((), (), s32[]{:S(2)}) async-start(), calls=%async_computation | async-start | bytes 17039360 | tf_op jit(solution)/shard_map/all_gather | solution.py:12
  14.0 352.2 %copy-start.1 = (f32[4,128,128]{2,1,0:T(8,128)S(1)}, f32[4,128,128]{2,1,0:T(8,128)}, u32[]{:S(2)}) copy-start(f32[4,128,128]{2,1,0:T(8,128)} %fusion.3) | copy-start | bytes 786436
Sparse Core Ops, SparseCore 0:
  11.7 144.5 all-gather.6
  159.9 138.0 all-gather.4
where the time goes:
time: 387 us; the launch traced here: 382 us
  waiting for transfers between devices  206 us (53%)
  other arithmetic  133 us (34%)
  matrix products  19 us (5%)
  between operations  14.2 us (4%)
  local copies, waits for them, and re-layouts  5.52 us (1%)
    all_gather x2, waiting for transfers between devices, carried_in(): everything = lax.all_gather(value, axis)  206 us
    select_n x128, other arithmetic, step(): return jnp.where(reached, new, before)  133 us
  transfers between devices with their start and end apart: 2, of which 2 were waited for; matrix products, arithmetic and copies ran while one was open for 21% of the time, Pallas kernels for 0%

commit v1 on v0

v1 whole, which is shorter than its diff:
```python
import functools

import jax
import jax.numpy as jnp
from jax import lax
from jax.experimental import pallas as pl
from jax.experimental.pallas import tpu as pltpu
from jax.sharding import PartitionSpec as P

DK = 128
RING = 8
MESH = pl.DeviceIdType.MESH
F32 = jnp.float32
BF16 = jnp.bfloat16
OFFSETS = (4, 3, 5, 2, 6, 1, 7)

NT = (((1,), (1,)), ((), ()))
NN = (((1,), (0,)), ((), ()))


def split(x):
    hi = x.astype(BF16)
    lo = (x - hi.astype(F32)).astype(BF16)
    return hi, lo


def left(x, axis):
    hi, lo = split(x)
    return jnp.concatenate([hi, lo, hi], axis=axis)


def right(x, axis):
    hi, lo = split(x)
    return jnp.concatenate([hi, hi, lo], axis=axis)


def product(a, b, dims):
    (ca,), (cb,) = dims[0]
    return lax.dot_general(left(a, ca), right(b, cb), dims, preferred_element_type=F32)


def kernel(heads, q_hbm, k_hbm, v_hbm, g_hbm, oq_hbm, ok_hbm, ov_hbm,
           q_v, k_v, v_v, g_v, aq, ak, av, local, row_in, row_out, total, col_in, back,
           load_sem, store_sem, send_sem, row_sem, col_sem, back_sem):
    me = lax.axis_index("seq")
    hd = lax.axis_index("head")
    z = lax.div(me, RING)
    y = lax.rem(me, RING)
    length = q_v.shape[1]
    part = DK // RING

    def in_row(d):
        return lax.rem(y + d, RING)

    def row_peer(d):
        return (z * RING + in_row(d), hd)

    def col_peer(d):
        return (lax.rem(z + d, RING) * RING + y, hd)

    barrier = pltpu.get_barrier_semaphore()
    for d in OFFSETS:
        pl.semaphore_signal(barrier, inc=1, device_id=row_peer(d), device_id_type=MESH)
        pl.semaphore_signal(barrier, inc=1, device_id=col_peer(d), device_id_type=MESH)

    def columns(h):
        return pl.ds(h * DK, DK)

    def load(i, h):
        hbm, vmem = ((k_hbm, k_v), (v_hbm, v_v), (q_hbm, q_v), (g_hbm, g_v))[i]
        return pltpu.make_async_copy(hbm.at[:, columns(h)], vmem.at[h], load_sem.at[i, h])

    for h in range(heads):
        for i in range(4):
            load(i, h).start()

    def send_row(h, d):
        return pltpu.make_async_remote_copy(
            src_ref=local.at[h, in_row(d)], dst_ref=row_in.at[h, y],
            send_sem=send_sem.at[0, h], recv_sem=row_sem.at[h], device_id=row_peer(d), device_id_type=MESH)

    def send_col(h, d):
        wrapped = lax.div(z + d, RING)
        return pltpu.make_async_remote_copy(
            src_ref=total.at[h, wrapped], dst_ref=col_in.at[h, d - 1],
            send_sem=send_sem.at[1, h], recv_sem=col_sem.at[h], device_id=col_peer(d), device_id_type=MESH)

    def send_back(h, d):
        return pltpu.make_async_remote_copy(
            src_ref=row_out.at[h, in_row(d)], dst_ref=back.at[h, y],
            send_sem=send_sem.at[2, h], recv_sem=back_sem.at[h], device_id=row_peer(d), device_id_type=MESH)

    def all_of(ref, count, sem):
        pltpu.make_async_copy(ref.at[pl.ds(0, count)], ref.at[pl.ds(0, count)], sem).wait()

    for h in range(heads):
        load(0, h).wait()
        load(1, h).wait()
        local[h, :, 0] = product(k_v[h].T, v_v[h], NN).reshape(RING, part, DK)
        load(2, h).wait()
        load(3, h).wait()
        local[h, :, 1] = product(q_v[h].T, g_v[h], NN).reshape(RING, part, DK)
        if h == 0:
            pl.semaphore_wait(barrier, 2 * (RING - 1))
        for d in OFFSETS:
            send_row(h, d).start()
        row_in[h, y] = local[h, y]

    rows = lax.broadcasted_iota(jnp.int32, (length, length), 0)
    cols = lax.broadcasted_iota(jnp.int32, (length, length), 1)
    for h in range(heads):
        q, k, v, g = q_v[h], k_v[h], v_v[h], g_v[h]
        scores_t = jnp.where(rows <= cols, product(k, q, NT), 0.0)
        av[h] = product(scores_t, g, NN)
        dscores = jnp.where(rows >= cols, product(g, v, NT), 0.0)
        aq[h] = product(dscores, k, NN)
        dscores_t = jnp.where(rows <= cols, product(v, g, NT), 0.0)
        ak[h] = product(dscores_t, q, NN)

    def row_step(h):
        all_of(row_in.at[h], RING - 1, row_sem.at[h])
        run = jnp.zeros((part, DK), F32)
        for j in range(RING):
            row_out[h, j, 0] = run
            run = run + row_in[h, j, 0]
        total[h, 0] = run
        run = jnp.zeros((part, DK), F32)
        for j in reversed(range(RING)):
            row_out[h, j, 1] = run
            run = run + row_in[h, j, 1]
        total[h, 1] = run
        for d in OFFSETS:
            send_col(h, d).start()

    def col_step(h):
        all_of(col_in.at[h], RING - 1, col_sem.at[h])
        earlier = jnp.zeros((part, DK), F32)
        later = jnp.zeros((part, DK), F32)
        for d in range(1, RING):
            came = col_in[h, d - 1]
            smaller = z >= d
            earlier = earlier + jnp.where(smaller, came, 0.0)
            later = later + jnp.where(smaller, 0.0, came)
        for j in range(RING):
            row_out[h, j, 0] = row_out[h, j, 0] + earlier
            row_out[h, j, 1] = row_out[h, j, 1] + later
        for d in OFFSETS:
            send_back(h, d).start()
        back[h, y] = row_out[h, y]

    def store(i, h):
        acc, hbm = ((aq, oq_hbm), (ak, ok_hbm), (av, ov_hbm))[i]
        return pltpu.make_async_copy(acc.at[h], hbm.at[:, columns(h)], store_sem.at[i, h])

    def last_step(h):
        all_of(back.at[h], RING - 1, back_sem.at[h])
        prefix = back[h, :, 0].reshape(DK, DK)
        suffix = back[h, :, 1].reshape(DK, DK)
        aq[h] = aq[h] + product(g_v[h], prefix, NT)
        store(0, h).start()
        ak[h] = ak[h] + product(v_v[h], suffix, NT)
        store(1, h).start()
        av[h] = av[h] + product(k_v[h], suffix, NN)
        store(2, h).start()

    lag = 2
    for step in range(heads + lag):
        if step < heads:
            row_step(step)
        if step >= lag:
            col_step(step - lag)
    for h in range(heads):
        last_step(h)
    for h in range(heads):
        for i in range(3):
            store(i, h).wait()
        all_of(local.at[h], RING - 1, send_sem.at[0, h])
        all_of(col_in.at[h], RING - 1, send_sem.at[1, h])
        all_of(row_out.at[h], RING - 1, send_sem.at[2, h])


def shards(queries, keys, values, out_grad):
    length, width = queries.shape
    heads = width // DK
    part = DK // RING
    out = jax.ShapeDtypeStruct((length, width), F32)
    block = pltpu.VMEM((heads, length, DK), F32)
    pieces = pltpu.VMEM((heads, RING, 2, part, DK), F32)
    return pl.pallas_call(
        functools.partial(kernel, heads),
        out_shape=(out, out, out),
        in_specs=[pl.BlockSpec(memory_space=pl.ANY)] * 4,
        out_specs=(pl.BlockSpec(memory_space=pl.ANY),) * 3,
        scratch_shapes=[block] * 7 + [
            pieces,
            pieces,
            pieces,
            pltpu.VMEM((heads, 2, part, DK), F32),
            pltpu.VMEM((heads, RING - 1, part, DK), F32),
            pieces,
            pltpu.SemaphoreType.DMA((4, heads)),
            pltpu.SemaphoreType.DMA((3, heads)),
            pltpu.SemaphoreType.DMA((3, heads)),
            pltpu.SemaphoreType.DMA((heads,)),
            pltpu.SemaphoreType.DMA((heads,)),
            pltpu.SemaphoreType.DMA((heads,)),
        ],
        compiler_params=pltpu.CompilerParams(
            collective_id=0, has_side_effects=True, vmem_limit_bytes=32 * 2**20),
        cost_estimate=pl.CostEstimate(
            flops=2 * 3 * heads * length * DK * (6 * length + 5 * DK),
            bytes_accessed=7 * 4 * length * width, transcendentals=0),
        name="linear_attention_backward",
    )(queries, keys, values, out_grad)


def solution(mesh):
    return jax.shard_map(
        shards,
        mesh=mesh,
        in_specs=(P("seq", "head"),) * 4,
        out_specs=(P("seq", "head"),) * 3,
        check_vma=False,
    )
```

time: 387 us -> 45.8 us (0.12); the launches traced: 382 us -> 45.5 us
  waiting for transfers between devices: 206 us -> 0 us
  other arithmetic: 133 us -> 0 us
  Pallas kernels: 0 us -> 38.3 us
  matrix products: 19 us -> 0 us
  between operations: 14.2 us -> 0.65 us
    all_gather x2 -> x0, waiting for transfers between devices: 206 us -> none  [carried_in(): everything = lax.all_gather(value, axis)]
    select_n x128 -> x0, other arithmetic: 133 us -> none  [step(): return jnp.where(reached, new, before)]
    pallas_call x0 -> x1, Pallas kernels: none -> 38.3 us  [shards(): pl.pallas_call(functools.partial(kernel, heads), out_shape=(out, out, out...]
    dot_general x10 -> x0, matrix products: 19 us -> none  [the longest x1 2.8 us: shards(): key_blocks = jnp.einsum('hnsd,hnse->hnde', k_blk, v_blk, precision=hi)]
  transfers between devices with their start and end apart: 2 -> 0, of which waited for: 2 -> 0; matrix products, arithmetic and copies ran while one was open for 21% -> 0% of each run, Pallas kernels for 0% -> 0%
where the time goes in v1:
time: 45.8 us; the launch traced here: 45.5 us
  Pallas kernels  38.3 us (84%)
  local copies, waits for them, and re-layouts  6.54 us (14%)
  between operations  0.65 us (1%)
    pallas_call x1, Pallas kernels, shards(): pl.pallas_call(functools.partial(kernel, heads), out_shape=(out, out, out...  38.3 us
    unnamed x11, local copies, waits for them, and re-layouts  6.54 us

profile of v1, /device:TPU:6, one launch (start us, length us, event | category | flops | bytes accessed | tf_op | source)
XLA Modules:
  0.0 45.5 jit_solution(3335550852739877620)
XLA Ops:
  0.6 0.0 copy-start
  0.6 1.0 %copy-done = f32[256,512]{1,0:T(8,128)S(1)} copy-done((f32[256,512]{1,0:T(8,128)S(1)}, f32[256,512]{1,0:T(8,128)}, u32[]{:S(2)}) %copy-start) | copy-done | bytes 524312
  1.7 0.0 copy-start.1
  1.7 1.0 %copy-done.1 = f32[256,512]{1,0:T(8,128)S(1)} copy-done((f32[256,512]{1,0:T(8,128)S(1)}, f32[256,512]{1,0:T(8,128)}, u32[]{:S(2)}) %copy-start.1) | copy-done | bytes 524312
  2.7 0.0 copy-start.2
  2.7 1.0 %copy-done.2 = f32[256,512]{1,0:T(8,128)S(1)} copy-done((f32[256,512]{1,0:T(8,128)S(1)}, f32[256,512]{1,0:T(8,128)}, u32[]{:S(2)}) %copy-start.2) | copy-done | bytes 524312
  3.8 0.0 copy-start.3
  3.8 1.0 %copy-done.3 = f32[256,512]{1,0:T(8,128)S(1)} copy-done((f32[256,512]{1,0:T(8,128)S(1)}, f32[256,512]{1,0:T(8,128)}, u32[]{:S(2)}) %copy-start.3) | copy-done | bytes 524312
  4.8 38.3 %linear_attention_backward.1 = (f32[256,512]{1,0:T(8,128)S(1)}, f32[256,512]{1,0:T(8,128)S(1)}, f32[256,512]{1,0:T(8,128)S(1)}) custom-call(f32[256,512]{1,0:T(8,128)S(1)} %copy-done, f32[256,512]{1,0:T(8,128)S(1)} %copy-done.1, f32[256,512]{1,0:T(8,128)S(1)} %copy-done.2, f32[256,512]{1,0:T(8,128)S(1)} %copy-done.3), custom_call_target="tpu_custom_call" | custom-call | flops 1711276032 | bytes 3670016 | tf_op jit(solution)/shard_map/linear_attention_backward/pallas_call | solution.py:189
  43.1 0.8 %copy.10 = f32[256,512]{1,0:T(8,128)} copy(f32[256,512]{1,0:T(8,128)S(1)} %get-tuple-element.6) | data formatting | bytes 1048576
  43.9 0.8 %copy.11 = f32[256,512]{1,0:T(8,128)} copy(f32[256,512]{1,0:T(8,128)S(1)} %get-tuple-element.7) | data formatting | bytes 1048576
  44.7 0.8 %copy.12 = f32[256,512]{1,0:T(8,128)} copy(f32[256,512]{1,0:T(8,128)S(1)} %get-tuple-element.8) | data formatting | bytes 1048576
Async XLA Ops:
  0.6 1.0 %copy-start = (f32[256,512]{1,0:T(8,128)S(1)}, f32[256,512]{1,0:T(8,128)}, u32[]{:S(2)}) copy-start(f32[256,512]{1,0:T(8,128)} %q_hbm.1) | copy-start | bytes 1572868
  1.7 1.0 %copy-start.1 = (f32[256,512]{1,0:T(8,128)S(1)}, f32[256,512]{1,0:T(8,128)}, u32[]{:S(2)}) copy-start(f32[256,512]{1,0:T(8,128)} %k_hbm.1) | copy-start | bytes 1572868
  2.7 1.0 %copy-start.2 = (f32[256,512]{1,0:T(8,128)S(1)}, f32[256,512]{1,0:T(8,128)}, u32[]{:S(2)}) copy-start(f32[256,512]{1,0:T(8,128)} %v_hbm.1) | copy-start | bytes 1572868
  3.8 1.0 %copy-start.3 = (f32[256,512]{1,0:T(8,128)S(1)}, f32[256,512]{1,0:T(8,128)}, u32[]{:S(2)}) copy-start(f32[256,512]{1,0:T(8,128)} %g_hbm.1) | copy-start | bytes 1572868

commit v2 on v1

v2 whole, which is shorter than its diff:
```python
import functools

import jax
import jax.numpy as jnp
from jax import lax
from jax.experimental import pallas as pl
from jax.experimental.pallas import tpu as pltpu
from jax.sharding import PartitionSpec as P

DK = 128
RING = 8
MESH = pl.DeviceIdType.MESH
F32 = jnp.float32
BF16 = jnp.bfloat16
OFFSETS = (4, 3, 5, 2, 6, 1, 7)
PER = 2

NT = (((1,), (1,)), ((), ()))
NN = (((1,), (0,)), ((), ()))


def split(x):
    hi = x.astype(BF16)
    lo = (x - hi.astype(F32)).astype(BF16)
    return hi, lo


def left(x, axis):
    hi, lo = split(x)
    return jnp.concatenate([hi, lo, hi], axis=axis)


def right(x, axis):
    hi, lo = split(x)
    return jnp.concatenate([hi, hi, lo], axis=axis)


def product(a, b, dims):
    (ca,), (cb,) = dims[0]
    return lax.dot_general(left(a, ca), right(b, cb), dims, preferred_element_type=F32)


def kernel(heads, q_hbm, k_hbm, v_hbm, g_hbm, aq, ak, av,
           q_v, k_v, v_v, g_v, local, row_in, row_out, total, col_in, back,
           load_sem, row_send, row_sem, col_send, col_sem, back_send, back_sem, ready):
    me = lax.axis_index("seq")
    hd = lax.axis_index("head")
    z = lax.div(me, RING)
    y = lax.rem(me, RING)
    length = q_v.shape[1]
    part = DK // RING
    chunks = heads // PER

    def in_row(d):
        return lax.rem(y + d, RING)

    def row_peer(d):
        return (z * RING + in_row(d), hd)

    def in_column(other):
        return (other * RING + y, hd)

    barrier = pltpu.get_barrier_semaphore()
    for d in OFFSETS:
        pl.semaphore_signal(barrier, inc=1, device_id=row_peer(d), device_id_type=MESH)

    def greet(d, _):
        pl.semaphore_signal(barrier, inc=1, device_id=in_column(z + d), device_id_type=MESH)
        return _

    lax.fori_loop(1, RING - z, greet, 0)

    def columns(h):
        return pl.ds(h * DK, DK)

    def load(i, h):
        hbm, vmem = ((k_hbm, k_v), (v_hbm, v_v), (q_hbm, q_v), (g_hbm, g_v))[i]
        return pltpu.make_async_copy(hbm.at[:, columns(h)], vmem.at[h], load_sem.at[i, h])

    def send_row(t, h, d):
        return pltpu.make_async_remote_copy(
            src_ref=local.at[t, h, in_row(d)], dst_ref=row_in.at[t, h, y],
            send_sem=row_send.at[t, h], recv_sem=row_sem.at[t, h], device_id=row_peer(d), device_id_type=MESH)

    def send_col(t, h, d):
        return pltpu.make_async_remote_copy(
            src_ref=total.at[t, h], dst_ref=col_in.at[t, h, d - 1],
            send_sem=col_send.at[t, h, d - 1], recv_sem=col_sem.at[t, h, d - 1],
            device_id=in_column(z - d if t else z + d), device_id_type=MESH)

    def send_back(t, h, d):
        return pltpu.make_async_remote_copy(
            src_ref=row_out.at[t, h, in_row(d)], dst_ref=back.at[t, h, y],
            send_sem=back_send.at[t, h], recv_sem=back_sem.at[t, h], device_id=row_peer(d), device_id_type=MESH)

    def all_of(ref, sem):
        some = ref.at[pl.ds(0, RING - 1)]
        pltpu.make_async_copy(some, some, sem).wait()

    def larger(t):
        return (z, RING - 1 - z) if t else (RING - 1 - z, z)

    def state(t, c):
        a, b = (q_v, g_v) if t else (k_v, v_v)
        for i in range(PER):
            h = c * PER + i
            load(2 * t, h).wait()
            load(2 * t + 1, h).wait()
            local[t, c, :, pl.ds(i * part, part)] = product(a[h].T, b[h], NN).reshape(RING, part, DK)

    def row_start(t, h):
        for d in OFFSETS:
            send_row(t, h, d).start()
        row_in[t, h, y] = local[t, h, y]

    def within(h):
        rows = lax.broadcasted_iota(jnp.int32, (length, length), 0)
        cols = lax.broadcasted_iota(jnp.int32, (length, length), 1)
        q, k, v, g = q_v[h], k_v[h], v_v[h], g_v[h]
        scores_t = jnp.where(rows <= cols, product(k, q, NT), 0.0)
        av[:, columns(h)] = product(scores_t, g, NN)
        dscores = jnp.where(rows >= cols, product(g, v, NT), 0.0)
        aq[:, columns(h)] = product(dscores, k, NN)
        dscores_t = jnp.where(rows <= cols, product(v, g, NT), 0.0)
        ak[:, columns(h)] = product(dscores_t, q, NN)

    def row_step(t, h):
        all_of(row_in.at[t, h], row_sem.at[t, h])
        run = jnp.zeros((PER * part, DK), F32)
        for j in (reversed(range(RING)) if t else range(RING)):
            row_out[t, h, j] = run
            run = run + row_in[t, h, j]
        total[t, h] = run
        if t == 0 and h == 0:

            @pl.when(z < RING - 1)
            def _():
                pl.semaphore_wait(ready, RING - 1 - z)

        count = larger(t)[0]

        def send(i, _):
            send_col(t, h, count - i).start()
            return _

        lax.fori_loop(0, count, send, 0)

    def col_step(t, h):
        def add(i, beyond):
            send_col(t, h, i + 1).wait_recv()
            return beyond + col_in[t, h, i]

        beyond = lax.fori_loop(0, larger(t)[1], add, jnp.zeros((PER * part, DK), F32))
        for j in range(RING):
            row_out[t, h, j] = row_out[t, h, j] + beyond
        for d in OFFSETS:
            send_back(t, h, d).start()
        back[t, h, y] = row_out[t, h, y]

    def last_step(t, c):
        all_of(back.at[t, c], back_sem.at[t, c])
        for i in range(PER):
            h = c * PER + i
            state = back[t, c, :, pl.ds(i * part, part)].reshape(DK, DK)
            if t:
                ak[:, columns(h)] = ak[:, columns(h)] + product(v_v[h], state, NT)
                av[:, columns(h)] = av[:, columns(h)] + product(k_v[h], state, NN)
            else:
                aq[:, columns(h)] = aq[:, columns(h)] + product(g_v[h], state, NT)

    def work(kinds, ahead, lag):
        order = [(t, c) for t in kinds for c in range(chunks)]
        for t in kinds:
            for h in range(heads):
                load(2 * t, h).start()
                load(2 * t + 1, h).start()
        for n, (t, c) in enumerate(order):
            state(t, c)
            if n == 0:
                pl.semaphore_wait(barrier, RING - 1 + z)

                def tell(d, _):
                    pl.semaphore_signal(ready, inc=1, device_id=in_column(z - d), device_id_type=MESH)
                    return _

                lax.fori_loop(1, z + 1, tell, 0)
            if n < ahead:
                row_start(t, c)
        for step in range(len(order) + lag):
            if step < chunks:
                for i in range(PER):
                    within(step * PER + i)
            if step < len(order):
                row_step(*order[step])
            if step + ahead < len(order):
                row_start(*order[step + ahead])
            if step >= lag:
                col_step(*order[step - lag])
        for t, c in order:
            last_step(t, c)

    @pl.when(z < RING // 2)
    def _():
        work((0, 1), 4, 2)

    @pl.when(z >= RING // 2)
    def _():
        work((1, 0), 4, 2)

    for t in range(2):
        for h in range(chunks):
            all_of(local.at[t, h], row_send.at[t, h])
            all_of(row_out.at[t, h], back_send.at[t, h])

            def sent(i, _):
                send_col(t, h, i + 1).wait_send()
                return _

            lax.fori_loop(0, larger(t)[0], sent, 0)


def write_out(aq, ak, av, oq, ok, ov, sem):
    slabs = sem.shape[1]
    rows = aq.shape[0] // slabs
    copies = []
    for i, (a, o) in enumerate(((aq, oq), (ak, ok), (av, ov))):
        for j in range(slabs):
            here = pl.ds(j * rows, rows)
            copies.append(pltpu.make_async_copy(a.at[here], o.at[here], sem.at[i, j]))
    for copy in copies:
        copy.start()
    for copy in copies:
        copy.wait()


def shards(queries, keys, values, out_grad):
    length, width = queries.shape
    heads = width // DK
    part = DK // RING
    chunks = heads // PER
    held = pltpu.VMEM((length, width), F32)
    out = pltpu.HBM((length, width), F32)
    arrays = [pltpu.with_memory_space_constraint(a, pltpu.HBM) for a in (queries, keys, values, out_grad)]
    block = pltpu.VMEM((heads, length, DK), F32)
    pieces = pltpu.VMEM((2, chunks, RING, PER * part, DK), F32)
    grads = pl.pallas_call(
        functools.partial(kernel, heads),
        out_shape=(held, held, held),
        in_specs=[pl.BlockSpec(memory_space=pltpu.HBM)] * 4,
        out_specs=(pl.BlockSpec(memory_space=pltpu.VMEM),) * 3,
        scratch_shapes=[block] * 4 + [
            pieces,
            pieces,
            pieces,
            pltpu.VMEM((2, chunks, PER * part, DK), F32),
            pltpu.VMEM((2, chunks, RING - 1, PER * part, DK), F32),
            pieces,
            pltpu.SemaphoreType.DMA((4, heads)),
            pltpu.SemaphoreType.DMA((2, chunks)),
            pltpu.SemaphoreType.DMA((2, chunks)),
            pltpu.SemaphoreType.DMA((2, chunks, RING - 1)),
            pltpu.SemaphoreType.DMA((2, chunks, RING - 1)),
            pltpu.SemaphoreType.DMA((2, chunks)),
            pltpu.SemaphoreType.DMA((2, chunks)),
            pltpu.SemaphoreType.REGULAR,
        ],
        compiler_params=pltpu.CompilerParams(
            collective_id=0, has_side_effects=True, vmem_limit_bytes=32 * 2**20),
        cost_estimate=pl.CostEstimate(
            flops=2 * 3 * heads * length * DK * (6 * length + 5 * DK),
            bytes_accessed=7 * 4 * length * width, transcendentals=0),
        name="linear_attention_backward",
    )(*arrays)
    return pl.pallas_call(
        write_out,
        out_shape=(out, out, out),
        in_specs=[pl.BlockSpec(memory_space=pltpu.VMEM)] * 3,
        out_specs=(pl.BlockSpec(memory_space=pltpu.HBM),) * 3,
        scratch_shapes=[pltpu.SemaphoreType.DMA((3, 4))],
        name="write_out",
    )(*[pltpu.with_memory_space_constraint(a, pltpu.VMEM) for a in grads])


def solution(mesh):
    return jax.shard_map(
        shards,
        mesh=mesh,
        in_specs=(P("seq", "head"),) * 4,
        out_specs=(P("seq", "head"),) * 3,
        check_vma=False,
    )
```

time: 45.8 us -> 36.7 us (0.80)
  local copies, waits for them, and re-layouts: 6.54 us -> 0 us
  Pallas kernels: 38.3 us -> 35.9 us
    unnamed x11 -> x0, local copies, waits for them, and re-layouts: 6.54 us -> none
    pallas_call x1 -> x2, Pallas kernels: 38.3 us -> 35.9 us  [the longest x1 34.6 us: shards(): pl.pallas_call(functools.partial(kernel, heads), out_shape=(held, held, h...]
where the time goes in v2:
time: 36.7 us; the launch traced here: 36.5 us
  Pallas kernels  35.9 us (98%)
  between operations  0.64 us (2%)
    pallas_call x1, Pallas kernels, shards(): pl.pallas_call(functools.partial(kernel, heads), out_shape=(held, held, h...  34.6 us
    pallas_call x1, Pallas kernels, shards(): pl.pallas_call(write_out, out_shape=(out, out, out), in_specs=[pl.BlockSp...  1.24 us

profile of v2, /device:TPU:6, one launch (start us, length us, event | category | flops | bytes accessed | tf_op | source)
XLA Modules:
  0.0 36.5 jit_solution(12982304963041039336)
XLA Ops:
  0.6 34.6 %linear_attention_backward.1 = (f32[256,512]{1,0:T(8,128)S(1)}, f32[256,512]{1,0:T(8,128)S(1)}, f32[256,512]{1,0:T(8,128)S(1)}) custom-call(f32[256,512]{1,0:T(8,128)} %q_hbm.1, f32[256,512]{1,0:T(8,128)} %k_hbm.1, f32[256,512]{1,0:T(8,128)} %v_hbm.1, f32[256,512]{1,0:T(8,128)} %g_hbm.1), custom_call_target="tpu_custom_call" | custom-call | flops 1711276032 | bytes 3670016 | tf_op jit(solution)/shard_map/linear_attention_backward/pallas_call | solution.py:246
  35.3 1.2 %write_out.1 = (f32[256,512]{1,0:T(8,128)}, f32[256,512]{1,0:T(8,128)}, f32[256,512]{1,0:T(8,128)}) custom-call(f32[256,512]{1,0:T(8,128)S(1)} %get-tuple-element.6.aq, f32[256,512]{1,0:T(8,128)S(1)} %get-tuple-element.7.ak, f32[256,512]{1,0:T(8,128)S(1)} %get-tuple-element.8.av), custom_call_target="tpu_custom_call" | custom-call | tf_op jit(solution)/shard_map/write_out/pallas_call | solution.py:274

commit v3 on v2

--- a/solution.py
+++ b/solution.py
@@ -12,7 +12,7 @@
 MESH = pl.DeviceIdType.MESH
 F32 = jnp.float32
 BF16 = jnp.bfloat16
-OFFSETS = (4, 3, 5, 2, 6, 1, 7)
+OFFSETS = (4, 3, 2, 1, 5, 6, 7)
 PER = 2
 
 NT = (((1,), (1,)), ((), ()))
@@ -35,13 +35,17 @@
     return jnp.concatenate([hi, hi, lo], axis=axis)
 
 
+def dot(a, b, dims):
+    return lax.dot_general(a, b, dims, preferred_element_type=F32)
+
+
 def product(a, b, dims):
     (ca,), (cb,) = dims[0]
-    return lax.dot_general(left(a, ca), right(b, cb), dims, preferred_element_type=F32)
+    return dot(left(a, ca), right(b, cb), dims)
 
 
 def kernel(heads, q_hbm, k_hbm, v_hbm, g_hbm, aq, ak, av,
-           q_v, k_v, v_v, g_v, local, row_in, row_out, total, col_in, back,
+           q_v, k_v, v_v, g_v, parts, local, row_in, row_out, total, col_in, back,
            load_sem, row_send, row_sem, col_send, col_sem, back_send, back_sem, ready):
     me = lax.axis_index("seq")
     hd = lax.axis_index("head")
@@ -52,7 +56,7 @@
     chunks = heads // PER
 
     def in_row(d):
-        return lax.rem(y + d, RING)
+        return lax.rem(y + jnp.where(lax.rem(hd, 2) == 0, d, RING - d), RING)
 
     def row_peer(d):
         return (z * RING + in_row(d), hd)
@@ -64,11 +68,21 @@
     for d in OFFSETS:
         pl.semaphore_signal(barrier, inc=1, device_id=row_peer(d), device_id_type=MESH)
 
-    def greet(d, _):
-        pl.semaphore_signal(barrier, inc=1, device_id=in_column(z + d), device_id_type=MESH)
-        return _
-
-    lax.fori_loop(1, RING - z, greet, 0)
+    def greet_column():
+        def greet(d, _):
+            pl.semaphore_signal(barrier, inc=1, device_id=in_column(z + d), device_id_type=MESH)
+            return _
+
+        lax.fori_loop(1, RING - z, greet, 0)
+
+    def meet():
+        pl.semaphore_wait(barrier, RING - 1 + z)
+
+        def tell(d, _):
+            pl.semaphore_signal(ready, inc=1, device_id=in_column(z - d), device_id_type=MESH)
+            return _
+
+        lax.fori_loop(1, z + 1, tell, 0)
 
     def columns(h):
         return pl.ds(h * DK, DK)
@@ -77,10 +91,11 @@
         hbm, vmem = ((k_hbm, k_v), (v_hbm, v_v), (q_hbm, q_v), (g_hbm, g_v))[i]
         return pltpu.make_async_copy(hbm.at[:, columns(h)], vmem.at[h], load_sem.at[i, h])
 
-    def send_row(t, h, d):
+    def send_row(t, c, d, first, count):
+        some = pl.ds(first * part, count * part)
         return pltpu.make_async_remote_copy(
-            src_ref=local.at[t, h, in_row(d)], dst_ref=row_in.at[t, h, y],
-            send_sem=row_send.at[t, h], recv_sem=row_sem.at[t, h], device_id=row_peer(d), device_id_type=MESH)
+            src_ref=local.at[t, c, in_row(d), some], dst_ref=row_in.at[t, c, y, some],
+            send_sem=row_send.at[t, c], recv_sem=row_sem.at[t, c], device_id=row_peer(d), device_id_type=MESH)
 
     def send_col(t, h, d):
         return pltpu.make_async_remote_copy(
@@ -100,28 +115,30 @@
     def larger(t):
         return (z, RING - 1 - z) if t else (RING - 1 - z, z)
 
-    def state(t, c):
+    def state(t, c, i):
         a, b = (q_v, g_v) if t else (k_v, v_v)
-        for i in range(PER):
-            h = c * PER + i
-            load(2 * t, h).wait()
-            load(2 * t + 1, h).wait()
-            local[t, c, :, pl.ds(i * part, part)] = product(a[h].T, b[h], NN).reshape(RING, part, DK)
-
-    def row_start(t, h):
+        h = c * PER + i
+        load(2 * t, h).wait()
+        load(2 * t + 1, h).wait()
+        local[t, c, :, pl.ds(i * part, part)] = product(a[h].T, b[h], NN).reshape(RING, part, DK)
+
+    def row_start(t, c, first, count):
         for d in OFFSETS:
-            send_row(t, h, d).start()
-        row_in[t, h, y] = local[t, h, y]
+            send_row(t, c, d, first, count).start()
 
     def within(h):
         rows = lax.broadcasted_iota(jnp.int32, (length, length), 0)
         cols = lax.broadcasted_iota(jnp.int32, (length, length), 1)
         q, k, v, g = q_v[h], k_v[h], v_v[h], g_v[h]
-        scores_t = jnp.where(rows <= cols, product(k, q, NT), 0.0)
+        k_left, v_left, g_left = left(k, 1), left(v, 1), left(g, 1)
+        parts[0, h] = k_left
+        parts[1, h] = v_left
+        parts[2, h] = g_left
+        scores_t = jnp.where(rows <= cols, dot(k_left, right(q, 1), NT), 0.0)
         av[:, columns(h)] = product(scores_t, g, NN)
-        dscores = jnp.where(rows >= cols, product(g, v, NT), 0.0)
+        dscores = jnp.where(rows >= cols, dot(g_left, right(v, 1), NT), 0.0)
         aq[:, columns(h)] = product(dscores, k, NN)
-        dscores_t = jnp.where(rows <= cols, product(v, g, NT), 0.0)
+        dscores_t = jnp.where(rows <= cols, dot(v_left, right(g, 1), NT), 0.0)
         ak[:, columns(h)] = product(dscores_t, q, NN)
 
     def row_step(t, h):
@@ -163,60 +180,65 @@
             h = c * PER + i
             state = back[t, c, :, pl.ds(i * part, part)].reshape(DK, DK)
             if t:
-                ak[:, columns(h)] = ak[:, columns(h)] + product(v_v[h], state, NT)
-                av[:, columns(h)] = av[:, columns(h)] + product(k_v[h], state, NN)
+                ak[:, columns(h)] = ak[:, columns(h)] + dot(parts[1, h], right(state, 1), NT)
+                av[:, columns(h)] = av[:, columns(h)] + dot(parts[0, h], right(state, 0), NN)
             else:
-                aq[:, columns(h)] = aq[:, columns(h)] + product(g_v[h], state, NT)
-
-    def work(kinds, ahead, lag):
+                aq[:, columns(h)] = aq[:, columns(h)] + dot(parts[2, h], right(state, 1), NT)
+
+    def all_sent(order):
+        for t, c in order:
+            all_of(local.at[t, c], row_send.at[t, c])
+            all_of(row_out.at[t, c], back_send.at[t, c])
+
+            def sent(i, _):
+                send_col(t, c, i + 1).wait_send()
+                return _
+
+            lax.fori_loop(0, larger(t)[0], sent, 0)
+
+    def work(kinds):
         order = [(t, c) for t in kinds for c in range(chunks)]
-        for t in kinds:
-            for h in range(heads):
-                load(2 * t, h).start()
-                load(2 * t + 1, h).start()
+
+        def load_chunk(t, c):
+            for i in range(PER):
+                load(2 * t, c * PER + i).start()
+                load(2 * t + 1, c * PER + i).start()
+
+        load_chunk(*order[0])
+        greet_column()
         for n, (t, c) in enumerate(order):
-            state(t, c)
-            if n == 0:
-                pl.semaphore_wait(barrier, RING - 1 + z)
-
-                def tell(d, _):
-                    pl.semaphore_signal(ready, inc=1, device_id=in_column(z - d), device_id_type=MESH)
-                    return _
-
-                lax.fori_loop(1, z + 1, tell, 0)
-            if n < ahead:
-                row_start(t, c)
+            for i in range(PER):
+                state(t, c, i)
+                if n == 0 and i == 0:
+                    for u, e in order[1:]:
+                        load_chunk(u, e)
+                    meet()
+                if n == 0:
+                    row_start(t, c, i, 1)
+            if n > 0:
+                row_start(t, c, 0, PER)
+            row_in[t, c, y] = local[t, c, y]
+        for h in range(heads):
+            within(h)
+        lag = 2
         for step in range(len(order) + lag):
-            if step < chunks:
-                for i in range(PER):
-                    within(step * PER + i)
             if step < len(order):
                 row_step(*order[step])
-            if step + ahead < len(order):
-                row_start(*order[step + ahead])
             if step >= lag:
                 col_step(*order[step - lag])
-        for t, c in order:
+        for t, c in order[:-1]:
             last_step(t, c)
+        all_sent(order[:-1])
+        last_step(*order[-1])
+        all_sent(order[-1:])
 
     @pl.when(z < RING // 2)
     def _():
-        work((0, 1), 4, 2)
+        work((0, 1))
 
     @pl.when(z >= RING // 2)
     def _():
-        work((1, 0), 4, 2)
-
-    for t in range(2):
-        for h in range(chunks):
-            all_of(local.at[t, h], row_send.at[t, h])
-            all_of(row_out.at[t, h], back_send.at[t, h])
-
-            def sent(i, _):
-                send_col(t, h, i + 1).wait_send()
-                return _
-
-            lax.fori_loop(0, larger(t)[0], sent, 0)
+        work((1, 0))
 
 
 def write_out(aq, ak, av, oq, ok, ov, sem):
@@ -249,6 +271,7 @@
         in_specs=[pl.BlockSpec(memory_space=pltpu.HBM)] * 4,
         out_specs=(pl.BlockSpec(memory_space=pltpu.VMEM),) * 3,
         scratch_shapes=[block] * 4 + [
+            pltpu.VMEM((3, heads, length, 3 * DK), BF16),
             pieces,
             pieces,
             pieces,
@@ -276,7 +299,7 @@
         out_shape=(out, out, out),
         in_specs=[pl.BlockSpec(memory_space=pltpu.VMEM)] * 3,
         out_specs=(pl.BlockSpec(memory_space=pltpu.HBM),) * 3,
-        scratch_shapes=[pltpu.SemaphoreType.DMA((3, 4))],
+        scratch_shapes=[pltpu.SemaphoreType.DMA((3, 1))],
         name="write_out",
     )(*[pltpu.with_memory_space_constraint(a, pltpu.VMEM) for a in grads])
 

time: 36.7 us -> 35.8 us (0.975)
  Pallas kernels: 35.9 us -> 35.1 us
    pallas_call x1, Pallas kernels: 34.6 us -> 33.9 us  [shards(): pl.pallas_call(functools.partial(kernel, heads), out_shape=(held, held, h...]
where the time goes in v3:
time: 35.8 us; the launch traced here: 35.7 us
  Pallas kernels  35.1 us (98%)
  between operations  0.64 us (2%)
    pallas_call x1, Pallas kernels, shards(): pl.pallas_call(functools.partial(kernel, heads), out_shape=(held, held, h...  33.9 us
    pallas_call x1, Pallas kernels, shards(): pl.pallas_call(write_out, out_shape=(out, out, out), in_specs=[pl.BlockSp...  1.17 us

profile of v3, /device:TPU:6, one launch (start us, length us, event | category | flops | bytes accessed | tf_op | source)
XLA Modules:
  0.0 35.7 jit_solution(9560161434431937172)
XLA Ops:
  0.6 33.9 %linear_attention_backward.1 = (f32[256,512]{1,0:T(8,128)S(1)}, f32[256,512]{1,0:T(8,128)S(1)}, f32[256,512]{1,0:T(8,128)S(1)}) custom-call(f32[256,512]{1,0:T(8,128)} %q_hbm.1, f32[256,512]{1,0:T(8,128)} %k_hbm.1, f32[256,512]{1,0:T(8,128)} %v_hbm.1, f32[256,512]{1,0:T(8,128)} %g_hbm.1), custom_call_target="tpu_custom_call" | custom-call | flops 1711276032 | bytes 3670016 | tf_op jit(solution)/shard_map/linear_attention_backward/pallas_call | solution.py:268
  34.5 1.2 %write_out.1 = (f32[256,512]{1,0:T(8,128)}, f32[256,512]{1,0:T(8,128)}, f32[256,512]{1,0:T(8,128)}) custom-call(f32[256,512]{1,0:T(8,128)S(1)} %get-tuple-element.6.aq, f32[256,512]{1,0:T(8,128)S(1)} %get-tuple-element.7.ak, f32[256,512]{1,0:T(8,128)S(1)} %get-tuple-element.8.av), custom_call_target="tpu_custom_call" | custom-call | tf_op jit(solution)/shard_map/write_out/pallas_call | solution.py:297

commit v4 on v3

--- a/solution.py
+++ b/solution.py
@@ -218,14 +218,28 @@
             if n > 0:
                 row_start(t, c, 0, PER)
             row_in[t, c, y] = local[t, c, y]
-        for h in range(heads):
+        core = lax.rem(hd, 2)
+        early = heads // 2
+        for h in range(early):
             within(h)
+
+        @pl.when(core == 1)
+        def _():
+            for h in range(early, heads):
+                within(h)
+
         lag = 2
         for step in range(len(order) + lag):
             if step < len(order):
                 row_step(*order[step])
             if step >= lag:
                 col_step(*order[step - lag])
+            if step == 0:
+                @pl.when(core == 0)
+                def _():
+                    for h in range(early, heads):
+                        within(h)
+
         for t, c in order[:-1]:
             last_step(t, c)
         all_sent(order[:-1])

time: 35.8 us -> 36.4 us (1.017)
  no operation moved by 1% of the time
where the time goes in v4:
time: 36.4 us; the launch traced here: 36.2 us
  Pallas kernels  35.4 us (97%)
  between operations  0.82 us (2%)
    pallas_call x1, Pallas kernels, shards(): pl.pallas_call(functools.partial(kernel, heads), out_shape=(held, held, h...  34.2 us
    pallas_call x1, Pallas kernels, shards(): pl.pallas_call(write_out, out_shape=(out, out, out), in_specs=[pl.BlockSp...  1.17 us

profile of v4, /device:TPU:6, one launch (start us, length us, event | category | flops | bytes accessed | tf_op | source)
XLA Modules:
  0.0 36.2 jit_solution(12025562672446619247)
XLA Ops:
  0.6 34.2 %linear_attention_backward.1 = (f32[256,512]{1,0:T(8,128)S(1)}, f32[256,512]{1,0:T(8,128)S(1)}, f32[256,512]{1,0:T(8,128)S(1)}) custom-call(f32[256,512]{1,0:T(8,128)} %q_hbm.1, f32[256,512]{1,0:T(8,128)} %k_hbm.1, f32[256,512]{1,0:T(8,128)} %v_hbm.1, f32[256,512]{1,0:T(8,128)} %g_hbm.1), custom_call_target="tpu_custom_call" | custom-call | flops 1711276032 | bytes 3670016 | tf_op jit(solution)/shard_map/linear_attention_backward/pallas_call | solution.py:282
  34.8 1.2 %write_out.1 = (f32[256,512]{1,0:T(8,128)}, f32[256,512]{1,0:T(8,128)}, f32[256,512]{1,0:T(8,128)}) custom-call(f32[256,512]{1,0:T(8,128)S(1)} %get-tuple-element.6.aq, f32[256,512]{1,0:T(8,128)S(1)} %get-tuple-element.7.ak, f32[256,512]{1,0:T(8,128)S(1)} %get-tuple-element.8.av), custom_call_target="tpu_custom_call" | custom-call | tf_op jit(solution)/shard_map/write_out/pallas_call | solution.py:311

commit v5 on v3

--- a/solution.py
+++ b/solution.py
@@ -78,6 +78,7 @@
     def meet():
         pl.semaphore_wait(barrier, RING - 1 + z)
 
+    def tell_column():
         def tell(d, _):
             pl.semaphore_signal(ready, inc=1, device_id=in_column(z - d), device_id_type=MESH)
             return _
@@ -210,11 +211,13 @@
             for i in range(PER):
                 state(t, c, i)
                 if n == 0 and i == 0:
-                    for u, e in order[1:]:
-                        load_chunk(u, e)
                     meet()
                 if n == 0:
                     row_start(t, c, i, 1)
+                if n == 0 and i == 0:
+                    for u, e in order[1:]:
+                        load_chunk(u, e)
+                    tell_column()
             if n > 0:
                 row_start(t, c, 0, PER)
             row_in[t, c, y] = local[t, c, y]

time: 35.8 us -> 36.6 us (1.022); the launches traced: 35.7 us -> 36 us
  no operation moved by 1% of the time
where the time goes in v5:
time: 36.6 us; the launch traced here: 36 us
  Pallas kernels  35.4 us (97%)
  between operations  0.64 us (2%)
    pallas_call x1, Pallas kernels, shards(): pl.pallas_call(functools.partial(kernel, heads), out_shape=(held, held, h...  34.2 us
    pallas_call x1, Pallas kernels, shards(): pl.pallas_call(write_out, out_shape=(out, out, out), in_specs=[pl.BlockSp...  1.17 us

profile of v5, /device:TPU:6, one launch (start us, length us, event | category | flops | bytes accessed | tf_op | source)
XLA Modules:
  0.0 36.0 jit_solution(1778325397770290314)
XLA Ops:
  0.6 34.2 %linear_attention_backward.1 = (f32[256,512]{1,0:T(8,128)S(1)}, f32[256,512]{1,0:T(8,128)S(1)}, f32[256,512]{1,0:T(8,128)S(1)}) custom-call(f32[256,512]{1,0:T(8,128)} %q_hbm.1, f32[256,512]{1,0:T(8,128)} %k_hbm.1, f32[256,512]{1,0:T(8,128)} %v_hbm.1, f32[256,512]{1,0:T(8,128)} %g_hbm.1), custom_call_target="tpu_custom_call" | custom-call | flops 1711276032 | bytes 3670016 | tf_op jit(solution)/shard_map/linear_attention_backward/pallas_call | solution.py:271
  34.8 1.2 %write_out.1 = (f32[256,512]{1,0:T(8,128)}, f32[256,512]{1,0:T(8,128)}, f32[256,512]{1,0:T(8,128)}) custom-call(f32[256,512]{1,0:T(8,128)S(1)} %get-tuple-element.6.aq, f32[256,512]{1,0:T(8,128)S(1)} %get-tuple-element.7.ak, f32[256,512]{1,0:T(8,128)S(1)} %get-tuple-element.8.av), custom_call_target="tpu_custom_call" | custom-call | tf_op jit(solution)/shard_map/write_out/pallas_call | solution.py:300
